TPU v7x, 256 devices: a whole 4x4x8 slice. The times are simulated.
256 devices in a mesh: head: 4 (over z_lo), blk: 64 (over x, y, z_hi, core).
Axes of the slice: x: 4, y: 4, z: 8 (z_hi: 2, z_lo: 4; z = z_hi * 4 + z_lo), core: 2. Of those that a mesh axis runs over, the one named last changes fastest.
Arguments:
- queries: bfloat16 [64, 512, 4096], P('blk', 'head'), may hold values from -6 to 6
- key_rows: bfloat16 [64, 512, 512], P('blk', 'head'), may hold values from -6 to 6
- value_rows: bfloat16 [64, 512, 512], P('blk', 'head'), may hold values from -6 to 6
- attn_out: bfloat16 [64, 512, 4096], P('blk', 'head'), may hold values from -6 to 6
- out_grad: bfloat16 [64, 512, 4096], P('blk', 'head'), may hold values from -3 to 3
- log_norm: float32 [64, 512, 32], P('blk', 'head'), may hold values from 5 to 7
- block_layout: int32 [128], replicated, may hold values from 0 to 127, each once
Outputs:
- query_grad: bfloat16 [64, 512, 4096], P('blk', 'head')
- key_grad: bfloat16 [64, 512, 512], P('blk', 'head')
- value_grad: bfloat16 [64, 512, 512], P('blk', 'head')
Inputs may be any that keep to these rules, and one draw needn't show every extreme that they name: Each block number stands once; the rows of blk index b are block block_layout[2 b] followed by block block_layout[2 b + 1].
All inputs are finite; a program needn't handle non-finite values.
Results may differ from a plain program's by a relative error of at most 0.014.
Values may be sent and summed in bfloat16 or wider, within the bound.
A program may use at most 128 MiB of HBM per device.

v0:
```python
import functools
import math

import jax
import jax.numpy as jnp
from jax import lax
from jax.experimental import pallas as pl
from jax.experimental.pallas import tpu as pltpu
from jax.sharding import PartitionSpec as P

HD = 128
GROUP = 8
KVH = 4
ROOT = math.sqrt(HD)
SCALE = 1.0 / ROOT
EXP2_SCALE = math.log2(math.e) / ROOT
BIG = 1e30
LINE = 4
MESH = pl.DeviceIdType.MESH
BF = jnp.bfloat16
F32 = jnp.float32


def nt(a, b):
    return lax.dot_general(a, b, (((1,), (1,)), ((), ())), preferred_element_type=F32)


def nn(a, b):
    return lax.dot_general(a, b, (((1,), (0,)), ((), ())), preferred_element_type=F32)


def tn(a, b):
    return lax.dot_general(a, b, (((0,), (0,)), ((), ())), preferred_element_type=F32)


def split3(x):
    hi = x.astype(BF).astype(F32)
    mid = (x - hi).astype(BF).astype(F32)
    return hi, mid, x - hi - mid


def kernel(
    n, layout, q_ref, k_hbm, v_hbm, o_ref, do_ref, lse_ref,
    dq_ref, dk_ref, dv_ref,
    lbuf, cbuf, sbuf, dbuf, aug, kcon, vcon, dq_t,
    part_l, part_c, out_s, out_d, out_c, out_l,
    in_s, in_d, in_c, in_x, in_r, in_w,
    sem_own, s_r, s_w, s_d, s_x, s_c, s_s, g_l, g_d, g_c, g_s,
    t_s, t_d, t_c, t_l, h_s, h_d, h_c, h_x, h_r, h_w,
):
    rows = q_ref.shape[1]
    b = lax.axis_index("blk")
    p = lax.axis_index("head")
    core = lax.rem(b, 2)

    def blk(i):
        return lax.rem(i + n, n)

    sib = b + 1 - 2 * core
    d_to = blk(b + 1 + 2 * core)
    d_from = blk(b - 3 + 2 * core)
    ahead = blk(b + 2)
    behind = blk(b - 2)

    def at(bb, pp):
        return {"blk": bb, "head": pp}

    def border(c, k):
        odd = lax.rem(k, 2)
        return jnp.where(odd == 1, (c + 3) // 2, c + c // 2)

    def both(*conds):
        out = conds[0]
        for c in conds[1:]:
            out = jnp.logical_and(out, c)
        return out

    def copy(src, dst, send, recv, dev):
        return pltpu.make_async_remote_copy(
            src_ref=src, dst_ref=dst, send_sem=send, recv_sem=recv,
            device_id=dev, device_id_type=MESH,
        )

    def c_right(k, u):
        return copy(lbuf.at[k, u], lbuf.at[k, u], s_r.at[k, u], g_l.at[k, u], at(b, p + 1))

    def c_left(k, u):
        return copy(lbuf.at[k, u], lbuf.at[k, u], s_w.at[k, u], g_l.at[k, u], at(b, p - 1))

    def c_d(k, u):
        return copy(lbuf.at[k, u], dbuf.at[k, u], s_d.at[k, u], g_d.at[k, u], at(d_to, p))

    def c_cross(k, u):
        return copy(lbuf.at[k, u], cbuf.at[k, u], s_x.at[k, u], g_c.at[k, u], at(ahead, 3 - p))

    def c_on(k, u, step):
        return copy(cbuf.at[k, u], cbuf.at[k, u], s_c.at[k, u], g_c.at[k, u], at(b, p + step))

    def c_sib(k, u):
        return copy(cbuf.at[k, u], sbuf.at[k, u], s_s.at[k, u], g_s.at[k, u], at(sib, p))

    def r_sib(k, u):
        return copy(out_s.at[k, u], in_s.at[k, u], t_s.at[k, u], h_s.at[k, u], at(sib, p))

    def r_d(k, u):
        return copy(out_d.at[k, u], in_d.at[k, u], t_d.at[k, u], h_d.at[k, u], at(d_from, p))

    def r_back(k, u, step):
        return copy(out_c.at[k, u], in_c.at[k, u], t_c.at[k, u], h_c.at[k, u], at(b, p + step))

    def r_cross(k, u):
        return copy(out_c.at[k, u], in_x.at[k, u], t_c.at[k, u], h_x.at[k, u], at(behind, 3 - p))

    def r_left(k, u):
        return copy(out_l.at[k, u], in_r.at[k, u], t_l.at[k, u], h_r.at[k, u], at(b, p - 1))

    def r_right(k, u):
        return copy(out_l.at[k, u], in_w.at[k, u], t_l.at[k, u], h_w.at[k, u], at(b, p + 1))

    def spread(k, u, act):
        pl.when(both(u <= p, p < LINE - 1))(lambda: act(c_right(k, u)))
        pl.when(both(u >= p, p > 0))(lambda: act(c_left(k, u)))
        over = jnp.logical_or(
            both(p == LINE - 1, u >= border(0, k)), both(p == 0, u < border(LINE - 1, k))
        )
        pl.when(over)(lambda: act(c_cross(k, u)))
        act(c_d(k, u))

    def pass_on(k, u, act):
        rising = u >= border(p, k)
        pl.when(both(rising, p < LINE - 1, u >= border(p + 1, k)))(lambda: act(c_on(k, u, 1)))
        pl.when(both(jnp.logical_not(rising), p > 0, u < border(p - 1, k)))(
            lambda: act(c_on(k, u, -1))
        )
        act(c_sib(k, u))

    start = lambda c: c.start()
    wait_send = lambda c: c.wait_send()

    def own_copy(k, part):
        src = (k_hbm, v_hbm)[part]
        lanes = pl.ds(pl.multiple_of(k * HD, HD), HD)
        return pltpu.make_async_copy(
            src.at[0, :, lanes], lbuf.at[k, p, part], sem_own.at[k, part]
        )

    def own_send(k):
        own_copy(k, 0).wait()
        own_copy(k, 1).wait()
        spread(k, p, start)

    def gather_gap(k, j):
        if j < LINE - 1:
            for u in (p - (j + 1), p + (j + 1)):
                @pl.when(both(u >= 0, u < LINE))
                def _(u=u):
                    c_right(k, u).wait_recv()
                    spread(k, u, start)
        up = 3 - (j - p)
        @pl.when(both(j >= p, up >= border(p, k)))
        def _():
            c_sib(k, up)
            c_on(k, up, 0).wait_recv()
            pass_on(k, up, start)
        down = j - (3 - p)
        @pl.when(both(down >= 0, down < border(p, k)))
        def _():
            c_on(k, down, 0).wait_recv()
            pass_on(k, down, start)

    def add(dst, src, k, u):
        dst[k, u] = dst[k, u] + src[k, u].astype(F32)

    def back_gap(k, j):
        def unit(u, rising):
            r_sib(k, u).wait_recv()
            add(part_c, in_s, k, u)
            if rising:
                more = both(p < LINE - 1, u >= border(p + 1, k))
            else:
                more = both(p > 0, u < border(p - 1, k))

            @pl.when(more)
            def _():
                r_back(k, u, 0).wait_recv()
                add(part_c, in_c, k, u)

            out_c[k, u] = part_c[k, u].astype(BF)
            send_back(k, u, rising, start)

        for u in range(LINE):
            pl.when(both(p == LINE - 1 - j, u >= border(p, k)))(lambda u=u: unit(u, True))
            pl.when(both(p == j, u < border(p, k)))(lambda u=u: unit(u, False))

    def send_back(k, u, rising, act):
        if rising:
            pl.when(p > 0)(lambda: act(r_back(k, u, -1)))
            pl.when(p == 0)(lambda: act(r_cross(k, u)))
        else:
            pl.when(p < LINE - 1)(lambda: act(r_back(k, u, 1)))
            pl.when(p == LINE - 1)(lambda: act(r_cross(k, u)))

    def sum_common(k, u):
        r_d(k, u).wait_recv()
        add(part_l, in_d, k, u)
        over = jnp.logical_or(
            both(p == LINE - 1, u >= border(0, k)), both(p == 0, u < border(LINE - 1, k))
        )

        @pl.when(over)
        def _():
            r_cross(k, u).wait_recv()
            add(part_l, in_x, k, u)

    def from_right(k, u):
        r_left(k, u).wait_recv()
        add(part_l, in_r, k, u)

    def from_left(k, u):
        r_right(k, u).wait_recv()
        add(part_l, in_w, k, u)

    def line_gap(k, j):
        def leftward(u):
            sum_common(k, u)
            pl.when(p < LINE - 1)(lambda: from_right(k, u))
            out_l[k, u] = part_l[k, u].astype(BF)
            r_left(k, u).start()

        def rightward(u):
            sum_common(k, u)
            pl.when(p > 0)(lambda: from_left(k, u))
            out_l[k, u] = part_l[k, u].astype(BF)
            r_right(k, u).start()

        for u in range(LINE):
            if j < LINE - 1:
                pl.when(both(p == LINE - 1 - j, u < p))(lambda u=u: leftward(u))
                pl.when(both(p == j, u > p))(lambda u=u: rightward(u))

    def finish(k):
        sum_common(k, p)
        pl.when(p < LINE - 1)(lambda: from_right(k, p))
        pl.when(p > 0)(lambda: from_left(k, p))
        lanes = pl.ds(pl.multiple_of(k * HD, HD), HD)
        dk_ref[0, :, lanes] = (part_l[k, p, 0] * SCALE).astype(BF)
        dv_ref[0, :, lanes] = part_l[k, p, 1].astype(BF)

    def prepare():
        lane = lax.broadcasted_iota(jnp.int32, (rows, HD), 1)

        def one(h, _):
            lanes = pl.ds(pl.multiple_of(h * HD, HD), HD)
            prod = do_ref[0, :, lanes].astype(F32) * o_ref[0, :, lanes].astype(F32)
            delta = jnp.sum(prod, axis=1, keepdims=True)
            which = lax.broadcasted_iota(jnp.int32, lse_ref.shape[1:], 1) == h
            lse = jnp.sum(jnp.where(which, lse_ref[0], 0.0), axis=1, keepdims=True) * ROOT
            w = jnp.where(lane == 3, 1.0, 0.0)
            for i, x in enumerate(split3(lse)):
                w = jnp.where(lane == i, x, w)
            for i, x in enumerate(split3(delta)):
                w = jnp.where(lane == 4 + i, x, w)
            aug[h] = w.astype(BF)
            return 0

        lax.fori_loop(0, KVH * GROUP, one, 0)
        vcon[...] = jnp.where(both(lane >= 4, lane < 7), -1.0, 0.0).astype(BF)
        mine = layout[2 * b + p // 2]
        for role, owner in enumerate((b, d_from, blk(sib - 2), behind)):
            for s in range(2):
                bias = jnp.where(layout[2 * owner + s] > mine, -BIG, 0.0)
                w = jnp.where(lane == 3, bias, jnp.where(lane < 3, -1.0, 0.0)).astype(BF)
                kcon[role, 2 * s] = w
                kcon[role, 2 * s + 1] = w

    keys_n = LINE * rows

    def chunk(k, role, buf):
        keys = buf[k, :, 0].reshape(keys_n, HD)
        vals = buf[k, :, 1].reshape(keys_n, HD)
        ka = jnp.concatenate([keys, kcon[role].reshape(keys_n, HD)], axis=1)
        va = jnp.concatenate([vals, jnp.concatenate([vcon[...]] * LINE, axis=0)], axis=1)
        qs, gs, qa, ga = [], [], [], []
        for g in range(GROUP):
            h = k * GROUP + g
            lanes = pl.ds(pl.multiple_of(h * HD, HD), HD)
            qs.append(q_ref[0, :, lanes])
            gs.append(do_ref[0, :, lanes])
            w = aug[h]
            qa.append(jnp.concatenate([qs[-1], w], axis=1))
            ga.append(jnp.concatenate([gs[-1], w], axis=1))
        qs, gs, qa, ga = [jnp.concatenate(x, axis=0) for x in (qs, gs, qa, ga)]
        st = nt(ka, qa)
        if role == 0:
            j = lax.broadcasted_iota(jnp.int32, st.shape, 0)
            t = lax.rem(lax.broadcasted_iota(jnp.int32, st.shape, 1), rows) + p * rows
            half = 2 * rows
            low = (p // 2) * half
            hidden = both(j > t, j >= low, j < low + half)
            st = jnp.where(hidden, -BIG, st)
        prob = jnp.exp2(st * EXP2_SCALE)
        ds = (prob * nt(va, ga)).astype(BF)
        dv = nn(prob.astype(BF), gs).reshape(LINE, rows, HD)
        dk = nn(ds, qs).reshape(LINE, rows, HD)
        dq = tn(keys, ds)
        if role == 0:
            dq_t[...] = dq
        else:
            dq_t[...] += dq
        return dk, dv

    def store(dst, k, dk, dv):
        dst[k, :, 0] = dk.astype(dst.dtype)
        dst[k, :, 1] = dv.astype(dst.dtype)

    def dq_out(k):
        for g in range(GROUP):
            lanes = pl.ds(pl.multiple_of((k * GROUP + g) * HD, HD), HD)
            tile = dq_t[:, g * rows:(g + 1) * rows] * SCALE
            dq_ref[0, :, lanes] = tile.T.astype(BF)

    for k in range(KVH):
        own_copy(k, 0).start()
        own_copy(k, 1).start()

    barrier = pltpu.get_barrier_semaphore()

    def greet(dev):
        pl.semaphore_signal(barrier, inc=1, device_id=dev, device_id_type=MESH)

    greet(at(sib, p))
    greet(at(blk(b + 3 - 6 * (1 - core)), p))
    pl.when(p > 0)(lambda: greet(at(b, p - 1)))
    pl.when(p < LINE - 1)(lambda: greet(at(b, p + 1)))
    at_end = jnp.logical_or(p == 0, p == LINE - 1)

    @pl.when(at_end)
    def _():
        greet(at(ahead, 3 - p))
        greet(at(behind, 3 - p))

    pl.semaphore_wait(barrier, jnp.where(at_end, 5, 4))

    own_send(0)
    prepare()
    own_send(1)
    for j in range(4):
        gather_gap(0, j)

    def gap(i, j):
        if isinstance(i, int):
            when = lambda cond, f: f() if cond else None
        else:
            when = lambda cond, f: pl.when(cond)(f)
        if j == 0:
            when(i < 2, lambda: own_send(i + 2))
        when(i < 3, lambda: gather_gap(i + 1, j))
        one = i >= 1 if not isinstance(i, int) else 1 <= i < 5
        two = i >= 2 if not isinstance(i, int) else 2 <= i < 6
        when(one, lambda: back_gap(i - 1, j))
        when(two, lambda: line_gap(i - 2, j))
        if j == 3:
            when(two, lambda: finish(i - 2))

    def head(k, _):
        gap(k, 0)
        dk, dv = chunk(k, 0, lbuf)
        store(part_l, k, dk, dv)
        gap(k, 1)
        for u in range(LINE):
            c_d(k, u).wait_recv()
        dk, dv = chunk(k, 1, dbuf)
        store(out_d, k, dk, dv)
        for u in range(LINE):
            r_d(k, u).start()
        gap(k, 2)
        for u in range(LINE):
            c_sib(k, u).wait_recv()
        dk, dv = chunk(k, 2, sbuf)
        store(out_s, k, dk, dv)
        for u in range(LINE):
            r_sib(k, u).start()
        gap(k, 3)
        dk, dv = chunk(k, 3, cbuf)
        store(part_c, k, dk, dv)
        dq_out(k)
        return 0

    lax.fori_loop(0, KVH, head, 0)
    for i in (4, 5):
        for j in range(4):
            gap(i, j)

    def drain(k, _):
        for u in range(LINE):
            spread(k, u, wait_send)
            pass_on(k, u, wait_send)
            r_d(k, u).wait_send()
            r_sib(k, u).wait_send()
            rising = u >= border(p, k)
            pl.when(rising)(lambda: send_back(k, u, True, wait_send))
            pl.when(jnp.logical_not(rising))(lambda: send_back(k, u, False, wait_send))
            pl.when(u < p)(lambda: r_left(k, u).wait_send())
            pl.when(u > p)(lambda: r_right(k, u).wait_send())
        return 0

    lax.fori_loop(0, KVH, drain, 0)


def solution(mesh):
    n = mesh.shape["blk"]
    vm = pl.BlockSpec(memory_space=pltpu.VMEM)
    anywhere = pl.BlockSpec(memory_space=pl.ANY)

    def shards(queries, key_rows, value_rows, attn_out, out_grad, log_norm, block_layout):
        rows = queries.shape[1]
        unit = (KVH, LINE, 2, rows, HD)
        sem = pltpu.SemaphoreType.DMA((KVH, LINE))
        return pl.pallas_call(
            functools.partial(kernel, n),
            out_shape=(
                jax.ShapeDtypeStruct(queries.shape, BF),
                jax.ShapeDtypeStruct(key_rows.shape, BF),
                jax.ShapeDtypeStruct(value_rows.shape, BF),
            ),
            in_specs=[
                pl.BlockSpec(memory_space=pltpu.SMEM), vm, anywhere, anywhere, vm, vm, vm,
            ],
            out_specs=(vm, vm, vm),
            scratch_shapes=[pltpu.VMEM(unit, BF)] * 4
            + [
                pltpu.VMEM((KVH * GROUP, rows, HD), BF),
                pltpu.VMEM((4, LINE, rows, HD), BF),
                pltpu.VMEM((rows, HD), BF),
                pltpu.VMEM((HD, GROUP * rows), F32),
            ]
            + [pltpu.VMEM(unit, F32)] * 2
            + [pltpu.VMEM(unit, BF)] * 4
            + [pltpu.VMEM(unit, BF)] * 6
            + [pltpu.SemaphoreType.DMA((KVH, 2))]
            + [sem] * 20,
            compiler_params=pltpu.CompilerParams(
                collective_id=0, has_side_effects=True, vmem_limit_bytes=56 * 2**20
            ),
        )(block_layout, queries, key_rows, value_rows, attn_out, out_grad, log_norm)

    placed = P("blk", "head", None)
    return jax.shard_map(
        shards,
        mesh=mesh,
        in_specs=(placed,) * 6 + (P(),),
        out_specs=(placed,) * 3,
        check_vma=False,
    )
```

profile of v0, /device:TPU:126, one launch (start us, length us, event | category | flops | bytes accessed | tf_op | source)
XLA Modules:
  0.0 122.6 jit_solution(9848404172500116880)
XLA Ops:
  0.6 1.4 %copy.10.lse_ref = f32[1,128,32]{2,1,0:T(8,128)} copy(f32[1,128,32]{1,2,0:T(8,128)} %param.12) | data formatting | bytes 32768 | tf_op args[5]
  2.1 116.6 %shard_map.94 = (bf16[1,128,4096]{2,1,0:T(8,128)(2,1)}, bf16[1,128,512]{2,1,0:T(8,128)(2,1)}, bf16[1,128,512]{2,1,0:T(8,128)(2,1)}) custom-call(s32[128]{0:T(128)} %layout.1, bf16[1,128,4096]{2,1,0:T(8,128)(2,1)} %q_ref.1, bf16[1,128,512]{2,1,0:T(8,128)(2,1)} %k_hbm.1, bf16[1,128,512]{2,1,0:T(8,128)(2,1)} %v_hbm.1, bf16[1,128,4096]{2,1,0:T(8,128)(2,1)} %o_ref.1, ...), custom_call_target="tpu_custom_call" | custom-call | tf_op jit(solution)/shard_map/pallas_call | solution.py:419
  118.7 0.0 copy-start.1
  118.7 2.3 %copy.14 = bf16[1,128,4096]{2,1,0:T(8,128)(2,1)} copy(bf16[1,128,4096]{2,1,0:T(8,128)(2,1)} %get-tuple-element.6) | data formatting | bytes 2097152
  121.0 0.0 copy-done.1
  121.0 0.0 copy-start
  121.0 0.7 copy.15
  121.7 0.3 copy-done
  122.0 0.7 copy.16
Async XLA Ops:
  118.7 2.3 %copy-start.1 = (bf16[1,128,512]{2,1,0:T(8,128)(2,1)S(1)}, bf16[1,128,512]{2,1,0:T(8,128)(2,1)}, u32[]{:S(2)}) copy-start(bf16[1,128,512]{2,1,0:T(8,128)(2,1)} %get-tuple-element.7) | copy-start | bytes 393220
  121.0 1.0 copy-start
where the time goes:
time: 123 us
  Pallas kernels  117 us (95%)
  local copies, waits for them, and re-layouts  5.38 us (4%)
    pallas_call x1, Pallas kernels, shards(): pl.pallas_call(functools.partial(kernel, n), out_shape=(jax.ShapeDtypeStr...  117 us
    unnamed x8, local copies, waits for them, and re-layouts  5.38 us

commit v1 on v0

v1 whole, which is shorter than its diff:
```python
import functools
import math

import jax
import jax.numpy as jnp
from jax import lax
from jax.experimental import pallas as pl
from jax.experimental.pallas import tpu as pltpu
from jax.sharding import PartitionSpec as P

HD = 128
GROUP = 8
KVH = 4
ROOT = math.sqrt(HD)
SCALE = 1.0 / ROOT
EXP2_SCALE = math.log2(math.e) / ROOT
BIG = 1e30
LINE = 4
REACH = ((1, 2, 2, 3), (0, 1, 3, 4))
MESH = pl.DeviceIdType.MESH
BF = jnp.bfloat16
F32 = jnp.float32


def nt(a, b):
    return lax.dot_general(a, b, (((1,), (1,)), ((), ())), preferred_element_type=F32)


def nn(a, b):
    return lax.dot_general(a, b, (((1,), (0,)), ((), ())), preferred_element_type=F32)


def tn(a, b):
    return lax.dot_general(a, b, (((0,), (0,)), ((), ())), preferred_element_type=F32)


def split3(x):
    hi = x.astype(BF).astype(F32)
    mid = (x - hi).astype(BF).astype(F32)
    return hi, mid, x - hi - mid


def kernel(
    n, layout, q_ref, k_hbm, v_hbm, o_ref, do_ref, lse_ref,
    dq_ref, dk_ref, dv_ref,
    got, aug, kcon, vcon, dq_t, part, acc, out_c, out_l,
    in_s, in_d, in_c, in_x, in_r, in_w,
    sem_own, s_r, s_w, s_x, s_c, s_d, s_s, g_l, g_c, g_d, g_s,
    t_c, t_l, t_s, t_d, h_c, h_x, h_r, h_w, h_s, h_d,
):
    rows = q_ref.shape[1]
    b = lax.axis_index("blk")
    p = lax.axis_index("head")
    core = lax.rem(b, 2)
    lbuf, dbuf, sbuf, cbuf = [got.at[role] for role in range(4)]

    def blk(i):
        return lax.rem(i + n, n)

    sib = b + 1 - 2 * core
    d_to = blk(b + 1 + 2 * core)
    d_from = blk(b - 3 + 2 * core)
    ahead = blk(b + 2)
    behind = blk(b - 2)

    def at(bb, pp):
        return {"blk": bb, "head": pp}

    def both(*conds):
        out = conds[0]
        for c in conds[1:]:
            out = jnp.logical_and(out, c)
        return out

    def reach(u, k):
        if isinstance(k, int):
            return REACH[k % 2][u]
        return jnp.where(lax.rem(k, 2) == 1, REACH[1][u], REACH[0][u])

    def copy(src, dst, send, recv, dev):
        return pltpu.make_async_remote_copy(
            src_ref=src, dst_ref=dst, send_sem=send, recv_sem=recv,
            device_id=dev, device_id_type=MESH,
        )

    def c_right(k, u):
        return copy(lbuf.at[k, u], lbuf.at[k, u], s_r.at[k, u], g_l.at[k, u], at(b, p + 1))

    def c_left(k, u):
        return copy(lbuf.at[k, u], lbuf.at[k, u], s_w.at[k, u], g_l.at[k, u], at(b, p - 1))

    def c_cross(k, u):
        return copy(lbuf.at[k, u], cbuf.at[k, u], s_x.at[k, u], g_c.at[k, u], at(ahead, 3 - p))

    def c_on(k, u, step):
        return copy(cbuf.at[k, u], cbuf.at[k, u], s_c.at[k, u], g_c.at[k, u], at(b, p + step))

    def c_d(k, u):
        return copy(lbuf.at[k, u], dbuf.at[k, u], s_d.at[k], g_d.at[k], at(d_to, p))

    def c_sib(k, u):
        return copy(cbuf.at[k, u], sbuf.at[k, u], s_s.at[k], g_s.at[k], at(sib, p))

    def c_d_all(k):
        return copy(lbuf.at[k], dbuf.at[k], s_d.at[k], g_d.at[k], at(d_to, p))

    def c_sib_all(k):
        return copy(cbuf.at[k], sbuf.at[k], s_s.at[k], g_s.at[k], at(sib, p))

    def r_sib(k):
        return copy(part.at[2, k], in_s.at[k], t_s.at[k], h_s.at[k], at(sib, p))

    def r_d(k):
        return copy(part.at[1, k], in_d.at[k], t_d.at[k], h_d.at[k], at(d_from, p))

    def r_back(k, u, step):
        return copy(out_c.at[k, u], in_c.at[k, u], t_c.at[k, u], h_c.at[k, u], at(b, p + step))

    def r_cross(k, u):
        return copy(out_c.at[k, u], in_x.at[k, u], t_c.at[k, u], h_x.at[k, u], at(behind, 3 - p))

    def r_left(k, u):
        return copy(out_l.at[k, u], in_r.at[k, u], t_l.at[k, u], h_r.at[k, u], at(b, p - 1))

    def r_right(k, u):
        return copy(out_l.at[k, u], in_w.at[k, u], t_l.at[k, u], h_w.at[k, u], at(b, p + 1))

    start = lambda c: c.start()
    wait_send = lambda c: c.wait_send()

    def crosses(k, u):
        return jnp.logical_or(
            both(p == LINE - 1, reach(u, k) > 0), both(p == 0, reach(u, k) < LINE)
        )

    def spread(k, u, act):
        pl.when(crosses(k, u))(lambda: act(c_cross(k, u)))
        pl.when(both(u <= p, p < LINE - 1))(lambda: act(c_right(k, u)))
        pl.when(both(u >= p, p > 0))(lambda: act(c_left(k, u)))

    def pass_on(k, u, act):
        top = reach(u, k)
        pl.when(p + 1 < top)(lambda: act(c_on(k, u, 1)))
        pl.when(p > top)(lambda: act(c_on(k, u, -1)))

    def own_copy(k, which):
        src = (k_hbm, v_hbm)[which]
        lanes = pl.ds(pl.multiple_of(k * HD, HD), HD)
        return pltpu.make_async_copy(
            src.at[0, :, lanes], lbuf.at[k, p, which], sem_own.at[k, which]
        )

    def own_send(k):
        own_copy(k, 0).wait()
        own_copy(k, 1).wait()
        for u in range(LINE):
            @pl.when(p == u)
            def _(u=u):
                spread(k, u, start)
                c_d(k, u).start()

    def gather(k, j):
        for u in range(LINE):
            if j < LINE - 1:
                @pl.when(jnp.logical_or(p - u == j + 1, u - p == j + 1))
                def _(u=u):
                    c_right(k, u).wait_recv()
                    spread(k, u, start)
                    c_d(k, u).start()

            top = reach(u, k)
            rise = both(p < top, p + (3 - u) == j)
            fall = both(p >= top, u + 3 - p == j)

            @pl.when(jnp.logical_or(rise, fall))
            def _(u=u):
                c_cross(k, u).wait_recv()
                pass_on(k, u, start)
                c_sib(k, u).start()

    def add(src, k, u):
        acc[...] += src[k, u].astype(F32)

    def send_back(k, u, act):
        top = reach(u, k)
        pl.when(both(p < top, p > 0))(lambda: act(r_back(k, u, -1)))
        pl.when(both(p >= top, p < LINE - 1))(lambda: act(r_back(k, u, 1)))
        pl.when(jnp.logical_or(both(p < top, p == 0), both(p >= top, p == LINE - 1)))(
            lambda: act(r_cross(k, u))
        )

    def line_terms(k, u):
        acc[...] = part[0, k, u].astype(F32)
        add(in_d, k, u)

        @pl.when(crosses(k, u))
        def _():
            r_cross(k, u).wait_recv()
            add(in_x, k, u)

    def from_right(k, u):
        r_left(k, u).wait_recv()
        add(in_r, k, u)

    def from_left(k, u):
        r_right(k, u).wait_recv()
        add(in_w, k, u)

    def finish(k, u):
        line_terms(k, u)
        pl.when(p < LINE - 1)(lambda: from_right(k, u))
        pl.when(p > 0)(lambda: from_left(k, u))
        lanes = pl.ds(pl.multiple_of(k * HD, HD), HD)
        dk_ref[0, :, lanes] = (acc[0] * SCALE).astype(BF)
        dv_ref[0, :, lanes] = acc[1].astype(BF)

    def back(k, t):
        if t == 0:
            r_sib(k).wait_recv()
        if t == 1:
            r_d(k).wait_recv()
        for u in range(LINE):
            top = reach(u, k)
            if t < LINE:
                last = jnp.logical_or(p == top - 1, p == top) if t == 0 else None
                turn = last if t == 0 else jnp.logical_or(p == top - 1 - t, p == top + t)

                @pl.when(turn)
                def _(u=u):
                    acc[...] = part[3, k, u].astype(F32)
                    add(in_s, k, u)
                    if t > 0:
                        r_back(k, u, 0).wait_recv()
                        add(in_c, k, u)
                    out_c[k, u] = acc[...].astype(BF)
                    send_back(k, u, start)

            if t > 0:
                @pl.when(both(p > u, jnp.maximum(1, top) + 3 - p == t))
                def _(u=u):
                    line_terms(k, u)
                    pl.when(p < LINE - 1)(lambda: from_right(k, u))
                    out_l[k, u] = acc[...].astype(BF)
                    r_left(k, u).start()

                @pl.when(both(p < u, jnp.maximum(1, LINE - top) + p == t))
                def _(u=u):
                    line_terms(k, u)
                    pl.when(p > 0)(lambda: from_left(k, u))
                    out_l[k, u] = acc[...].astype(BF)
                    r_right(k, u).start()

            if t == LINE:
                pl.when(p == u)(lambda u=u: finish(k, u))

    def prepare():
        lane = lax.broadcasted_iota(jnp.int32, (rows, HD), 1)
        lses = lse_ref[0].T * ROOT
        heads = lax.broadcasted_iota(jnp.int32, lses.shape, 1)

        def one(h, _):
            lanes = pl.ds(pl.multiple_of(h * HD, HD), HD)
            prod = do_ref[0, :, lanes].astype(F32) * o_ref[0, :, lanes].astype(F32)
            delta = jnp.sum(prod, axis=1, keepdims=True)
            lse = jnp.sum(jnp.where(heads == h, lses, 0.0), axis=1, keepdims=True)
            w = jnp.where(lane == 3, 1.0, 0.0)
            for i, x in enumerate(split3(lse)):
                w = jnp.where(lane == i, x, w)
            for i, x in enumerate(split3(delta)):
                w = jnp.where(lane == 4 + i, x, w)
            aug[h] = w.astype(BF)
            return 0

        lax.fori_loop(0, KVH * GROUP, one, 0)
        vcon[...] = jnp.where(both(lane >= 4, lane < 7), -1.0, 0.0).astype(BF)
        dq_t[...] = jnp.zeros_like(dq_t)
        mine = layout[2 * b + p // 2]
        for role, owner in enumerate((b, d_from, blk(sib - 2), behind)):
            for s in range(2):
                bias = jnp.where(layout[2 * owner + s] > mine, -BIG, 0.0)
                w = jnp.where(lane == 3, bias, jnp.where(lane < 3, -1.0, 0.0)).astype(BF)
                kcon[role, 2 * s] = w
                kcon[role, 2 * s + 1] = w

    keys_n = LINE * rows

    def chunk(k, role, own):
        keys = got[role, k, :, 0].reshape(keys_n, HD)
        vals = got[role, k, :, 1].reshape(keys_n, HD)
        ka = jnp.concatenate([keys, kcon[role].reshape(keys_n, HD)], axis=1)
        va = jnp.concatenate([vals, jnp.concatenate([vcon[...]] * LINE, axis=0)], axis=1)
        qs, gs, qa, ga = [], [], [], []
        for g in range(GROUP):
            h = k * GROUP + g
            lanes = pl.ds(pl.multiple_of(h * HD, HD), HD)
            qs.append(q_ref[0, :, lanes])
            gs.append(do_ref[0, :, lanes])
            w = aug[h]
            qa.append(jnp.concatenate([qs[-1], w], axis=1))
            ga.append(jnp.concatenate([gs[-1], w], axis=1))
        qs, gs, qa, ga = [jnp.concatenate(x, axis=0) for x in (qs, gs, qa, ga)]
        st = nt(ka, qa)
        if own:
            j = lax.broadcasted_iota(jnp.int32, st.shape, 0)
            t = lax.rem(lax.broadcasted_iota(jnp.int32, st.shape, 1), rows) + p * rows
            half = 2 * rows
            low = (p // 2) * half
            hidden = both(j > t, j >= low, j < low + half)
            st = jnp.where(hidden, -BIG, st)
        prob = jnp.exp2(st * EXP2_SCALE)
        ds = (prob * nt(va, ga)).astype(BF)
        part[role, k, :, 1] = nn(prob.astype(BF), gs).reshape(LINE, rows, HD).astype(BF)
        part[role, k, :, 0] = nn(ds, qs).reshape(LINE, rows, HD).astype(BF)
        dq_t[...] += tn(keys, ds)

    def dq_out(k):
        for g in range(GROUP):
            lanes = pl.ds(pl.multiple_of((k * GROUP + g) * HD, HD), HD)
            tile = dq_t[:, g * rows:(g + 1) * rows] * SCALE
            dq_ref[0, :, lanes] = tile.T.astype(BF)
        dq_t[...] = jnp.zeros_like(dq_t)

    for k in range(KVH):
        own_copy(k, 0).start()
        own_copy(k, 1).start()

    barrier = pltpu.get_barrier_semaphore()

    def greet(dev):
        pl.semaphore_signal(barrier, inc=1, device_id=dev, device_id_type=MESH)

    greet(at(sib, p))
    greet(at(blk(b + 3 - 6 * (1 - core)), p))
    pl.when(p > 0)(lambda: greet(at(b, p - 1)))
    pl.when(p < LINE - 1)(lambda: greet(at(b, p + 1)))
    at_end = jnp.logical_or(p == 0, p == LINE - 1)

    @pl.when(at_end)
    def _():
        greet(at(ahead, 3 - p))
        greet(at(behind, 3 - p))

    pl.semaphore_wait(barrier, jnp.where(at_end, 5, 4))

    own_send(0)
    prepare()
    gather(0, 0)
    own_send(1)
    gather(0, 1)
    gather(1, 0)
    gather(0, 2)

    def when(cond, f):
        pl.when(cond)(f)

    def step(c, _):
        i = lax.div(c, 4)
        s = lax.rem(c, 4)

        @pl.when(s == 0)
        def _():
            when(i < 3, lambda: gather(i + 1, 1))
            when(i == 1, lambda: back(0, 0))

        @pl.when(s == 1)
        def _():
            when(i == 0, lambda: gather(0, 3))
            when(i < 3, lambda: gather(i + 1, 2))
            when(i < 2, lambda: own_send(i + 2))
            when(i >= 1, lambda: back(i - 1, 1))
            when(i >= 2, lambda: back(i - 2, 3))

        @pl.when(s == 3)
        def _():
            when(i < 3, lambda: gather(i + 1, 3))
            when(i < 2, lambda: gather(i + 2, 0))
            when(i >= 1, lambda: back(i, 0))
            when(i >= 1, lambda: back(i - 1, 2))
            when(i >= 2, lambda: back(i - 2, 4))

        role = jnp.where(i == 0, s, jnp.where(s < 2, s + 2, 3 - s))
        when(role == 1, lambda: c_d_all(i).wait_recv())
        when(role == 2, lambda: c_sib_all(i).wait_recv())
        when(role == 0, lambda: chunk(i, 0, True))
        when(role > 0, lambda: chunk(i, role, False))
        when(role == 1, lambda: r_d(i).start())
        when(role == 2, lambda: r_sib(i).start())
        when(s == 3, lambda: dq_out(i))
        return 0

    lax.fori_loop(0, 4 * KVH, step, 0)
    back(3, 1)
    back(2, 3)
    back(3, 2)
    back(2, 4)
    back(3, 3)
    back(3, 4)

    def drain(k, _):
        for u in range(LINE):
            spread(k, u, wait_send)
            pass_on(k, u, wait_send)
            send_back(k, u, wait_send)
            pl.when(u < p)(lambda: r_left(k, u).wait_send())
            pl.when(u > p)(lambda: r_right(k, u).wait_send())
        c_d_all(k).wait_send()
        c_sib_all(k).wait_send()
        r_d(k).wait_send()
        r_sib(k).wait_send()
        return 0

    lax.fori_loop(0, KVH, drain, 0)


def solution(mesh):
    n = mesh.shape["blk"]
    vm = pl.BlockSpec(memory_space=pltpu.VMEM)
    anywhere = pl.BlockSpec(memory_space=pl.ANY)

    def shards(queries, key_rows, value_rows, attn_out, out_grad, log_norm, block_layout):
        rows = queries.shape[1]
        unit = (KVH, LINE, 2, rows, HD)
        sem = pltpu.SemaphoreType.DMA((KVH, LINE))
        sems = pltpu.SemaphoreType.DMA((KVH,))
        log_norm = jnp.transpose(log_norm, (0, 2, 1))
        return pl.pallas_call(
            functools.partial(kernel, n),
            out_shape=(
                jax.ShapeDtypeStruct(queries.shape, BF),
                jax.ShapeDtypeStruct(key_rows.shape, BF),
                jax.ShapeDtypeStruct(value_rows.shape, BF),
            ),
            in_specs=[
                pl.BlockSpec(memory_space=pltpu.SMEM), vm, anywhere, anywhere, vm, vm, vm,
            ],
            out_specs=(vm, vm, vm),
            scratch_shapes=[
                pltpu.VMEM((4,) + unit, BF),
                pltpu.VMEM((KVH * GROUP, rows, HD), BF),
                pltpu.VMEM((4, LINE, rows, HD), BF),
                pltpu.VMEM((rows, HD), BF),
                pltpu.VMEM((HD, GROUP * rows), F32),
                pltpu.VMEM((4,) + unit, BF),
                pltpu.VMEM((2, rows, HD), F32),
            ]
            + [pltpu.VMEM(unit, BF)] * 8
            + [pltpu.SemaphoreType.DMA((KVH, 2))]
            + [sem] * 4 + [sems] * 2 + [sem] * 2 + [sems] * 2
            + [sem] * 2 + [sems] * 2 + [sem] * 4 + [sems] * 2,
            compiler_params=pltpu.CompilerParams(
                collective_id=0, has_side_effects=True, vmem_limit_bytes=56 * 2**20
            ),
        )(block_layout, queries, key_rows, value_rows, attn_out, out_grad, log_norm)

    placed = P("blk", "head", None)
    return jax.shard_map(
        shards,
        mesh=mesh,
        in_specs=(placed,) * 6 + (P(),),
        out_specs=(placed,) * 3,
        check_vma=False,
    )
```

time: 123 us -> 92.9 us (0.76)
  the two profiles are of different devices: /device:TPU:126 before, /device:TPU:1 now
where the time goes in v1:
time: 92.9 us; the launch traced here: 91 us
  Pallas kernels  86.5 us (93%)
  local copies, waits for them, and re-layouts  3.93 us (4%)
    pallas_call x1, Pallas kernels, shards(): pl.pallas_call(functools.partial(kernel, n), out_shape=(jax.ShapeDtypeStr...  86.5 us
    unnamed x7, local copies, waits for them, and re-layouts  3.93 us

profile of v1, /device:TPU:1, one launch (start us, length us, event | category | flops | bytes accessed | tf_op | source)
XLA Modules:
  0.0 91.0 jit_solution(10289566595766352460)
XLA Ops:
  0.6 86.5 %shard_map.94 = (bf16[1,128,4096]{2,1,0:T(8,128)(2,1)}, bf16[1,128,512]{2,1,0:T(8,128)(2,1)}, bf16[1,128,512]{2,1,0:T(8,128)(2,1)}) custom-call(s32[128]{0:T(128)} %layout.1, bf16[1,128,4096]{2,1,0:T(8,128)(2,1)} %q_ref.1, bf16[1,128,512]{2,1,0:T(8,128)(2,1)} %k_hbm.1, bf16[1,128,512]{2,1,0:T(8,128)(2,1)} %v_hbm.1, bf16[1,128,4096]{2,1,0:T(8,128)(2,1)} %o_ref.1, ...), custom_call_target="tpu_custom_call" | custom-call | tf_op jit(solution)/shard_map/pallas_call | solution.py:426
  87.1 0.0 copy-start.1
  87.1 2.3 %copy.13 = bf16[1,128,4096]{2,1,0:T(8,128)(2,1)} copy(bf16[1,128,4096]{2,1,0:T(8,128)(2,1)} %get-tuple-element.6) | data formatting | bytes 2097152
  89.4 0.0 copy-done.1
  89.4 0.0 copy-start
  89.4 0.7 copy.14
  90.1 0.3 copy-done
  90.4 0.7 copy.15
Async XLA Ops:
  87.1 2.3 %copy-start.1 = (bf16[1,128,512]{2,1,0:T(8,128)(2,1)S(1)}, bf16[1,128,512]{2,1,0:T(8,128)(2,1)}, u32[]{:S(2)}) copy-start(bf16[1,128,512]{2,1,0:T(8,128)(2,1)} %get-tuple-element.7) | copy-start | bytes 393220
  89.4 1.0 %copy-start = (bf16[1,128,512]{2,1,0:T(8,128)(2,1)S(1)}, bf16[1,128,512]{2,1,0:T(8,128)(2,1)}, u32[]{:S(2)}) copy-start(bf16[1,128,512]{2,1,0:T(8,128)(2,1)} %get-tuple-element.8) | copy-start | bytes 393220

commit v2 on v1

--- a/solution.py
+++ b/solution.py
@@ -16,7 +16,9 @@
 EXP2_SCALE = math.log2(math.e) / ROOT
 BIG = 1e30
 LINE = 4
-REACH = ((1, 2, 2, 3), (0, 1, 3, 4))
+REACH = (0, 1, 3, 4)
+REACH_LAST = (1, 2, 2, 3)
+LAST = KVH - 1
 MESH = pl.DeviceIdType.MESH
 BF = jnp.bfloat16
 F32 = jnp.float32
@@ -41,14 +43,14 @@
 
 
 def kernel(
-    n, layout, q_ref, k_hbm, v_hbm, o_ref, do_ref, lse_ref,
-    dq_ref, dk_ref, dv_ref,
-    got, aug, kcon, vcon, dq_t, part, acc, out_c, out_l,
-    in_s, in_d, in_c, in_x, in_r, in_w,
+    n, layout, q_hbm, k_hbm, v_hbm, o_hbm, do_hbm, lse_ref,
+    dq_hbm, dk_ref, dv_ref,
+    q_ref, o_ref, do_ref, dq_ref, sem_in, sem_out, got, aug, kcon, vcon, kept, part, acc, out_c, out_l,
+    in_s, in_d, in_c, in_x, in_r, in_w, in_u,
     sem_own, s_r, s_w, s_x, s_c, s_d, s_s, g_l, g_c, g_d, g_s,
-    t_c, t_l, t_s, t_d, h_c, h_x, h_r, h_w, h_s, h_d,
+    t_c, t_l, t_s, t_d, h_c, h_x, h_r, h_w, h_s, h_d, h_u,
 ):
-    rows = q_ref.shape[1]
+    rows = q_ref.shape[0]
     b = lax.axis_index("blk")
     p = lax.axis_index("head")
     core = lax.rem(b, 2)
@@ -74,8 +76,8 @@
 
     def reach(u, k):
         if isinstance(k, int):
-            return REACH[k % 2][u]
-        return jnp.where(lax.rem(k, 2) == 1, REACH[1][u], REACH[0][u])
+            return REACH_LAST[u] if k % 2 == 1 else REACH[u]
+        return jnp.where(lax.rem(k, 2) == 1, REACH_LAST[u], REACH[u])
 
     def copy(src, dst, send, recv, dev):
         return pltpu.make_async_remote_copy(
@@ -95,9 +97,6 @@
     def c_on(k, u, step):
         return copy(cbuf.at[k, u], cbuf.at[k, u], s_c.at[k, u], g_c.at[k, u], at(b, p + step))
 
-    def c_d(k, u):
-        return copy(lbuf.at[k, u], dbuf.at[k, u], s_d.at[k], g_d.at[k], at(d_to, p))
-
     def c_sib(k, u):
         return copy(cbuf.at[k, u], sbuf.at[k, u], s_s.at[k], g_s.at[k], at(sib, p))
 
@@ -124,6 +123,9 @@
 
     def r_right(k, u):
         return copy(out_l.at[k, u], in_w.at[k, u], t_l.at[k, u], h_w.at[k, u], at(b, p + 1))
+
+    def r_owner(u, place):
+        return copy(out_l.at[LAST, u], in_u.at[place], t_l.at[LAST, u], h_u.at[place], at(b, u))
 
     start = lambda c: c.start()
     wait_send = lambda c: c.wait_send()
@@ -157,7 +159,6 @@
             @pl.when(p == u)
             def _(u=u):
                 spread(k, u, start)
-                c_d(k, u).start()
 
     def gather(k, j):
         for u in range(LINE):
@@ -166,7 +167,6 @@
                 def _(u=u):
                     c_right(k, u).wait_recv()
                     spread(k, u, start)
-                    c_d(k, u).start()
 
             top = reach(u, k)
             rise = both(p < top, p + (3 - u) == j)
@@ -210,31 +210,36 @@
         line_terms(k, u)
         pl.when(p < LINE - 1)(lambda: from_right(k, u))
         pl.when(p > 0)(lambda: from_left(k, u))
+        write_out(k)
+
+    def write_out(k):
         lanes = pl.ds(pl.multiple_of(k * HD, HD), HD)
-        dk_ref[0, :, lanes] = (acc[0] * SCALE).astype(BF)
-        dv_ref[0, :, lanes] = acc[1].astype(BF)
+        dk_ref[0, :, lanes] = (acc[0] * (2 * SCALE)).astype(BF)
+        dv_ref[0, :, lanes] = (acc[1] * 2.0).astype(BF)
+
+    def line_ahead(k, t):
+        for u in range(LINE):
+            top = reach(u, k)
+
+            @pl.when(jnp.logical_or(p == top - 1 - t, p == top + t))
+            def _(u=u):
+                acc[...] = part[3, k, u].astype(F32)
+                add(in_s, k, u)
+                if t > 0:
+                    r_back(k, u, 0).wait_recv()
+                    add(in_c, k, u)
+                out_c[k, u] = acc[...].astype(BF)
+                send_back(k, u, start)
 
     def back(k, t):
         if t == 0:
             r_sib(k).wait_recv()
         if t == 1:
             r_d(k).wait_recv()
+        if t < LINE:
+            line_ahead(k, t)
         for u in range(LINE):
             top = reach(u, k)
-            if t < LINE:
-                last = jnp.logical_or(p == top - 1, p == top) if t == 0 else None
-                turn = last if t == 0 else jnp.logical_or(p == top - 1 - t, p == top + t)
-
-                @pl.when(turn)
-                def _(u=u):
-                    acc[...] = part[3, k, u].astype(F32)
-                    add(in_s, k, u)
-                    if t > 0:
-                        r_back(k, u, 0).wait_recv()
-                        add(in_c, k, u)
-                    out_c[k, u] = acc[...].astype(BF)
-                    send_back(k, u, start)
-
             if t > 0:
                 @pl.when(both(p > u, jnp.maximum(1, top) + 3 - p == t))
                 def _(u=u):
@@ -253,14 +258,40 @@
             if t == LINE:
                 pl.when(p == u)(lambda u=u: finish(k, u))
 
-    def prepare():
+    def back_last(t):
+        if t == 1:
+            r_d(LAST).wait_recv()
+        if t < LINE - 1:
+            line_ahead(LAST, t)
+        for u in range(LINE):
+            top = REACH_LAST[u]
+            turn = jnp.where(p == LINE - 1, max(1, top), jnp.where(p == 0, max(1, LINE - top), 1))
+
+            @pl.when(both(p != u, turn == t))
+            def _(u=u):
+                line_terms(LAST, u)
+                out_l[LAST, u] = acc[...].astype(BF)
+                r_owner(u, p).start()
+
+        if t == LINE - 1:
+            for u in range(LINE):
+                @pl.when(p == u)
+                def _(u=u):
+                    line_terms(LAST, u)
+                    for place in range(LINE):
+                        if place != u:
+                            r_owner((u + 1) % LINE, place).wait_recv()
+                            acc[...] += in_u[place].astype(F32)
+                    write_out(LAST)
+
+    def prepare(k):
         lane = lax.broadcasted_iota(jnp.int32, (rows, HD), 1)
         lses = lse_ref[0].T * ROOT
         heads = lax.broadcasted_iota(jnp.int32, lses.shape, 1)
 
         def one(h, _):
             lanes = pl.ds(pl.multiple_of(h * HD, HD), HD)
-            prod = do_ref[0, :, lanes].astype(F32) * o_ref[0, :, lanes].astype(F32)
+            prod = do_ref[:, lanes].astype(F32) * o_ref[:, lanes].astype(F32)
             delta = jnp.sum(prod, axis=1, keepdims=True)
             lse = jnp.sum(jnp.where(heads == h, lses, 0.0), axis=1, keepdims=True)
             w = jnp.where(lane == 3, 1.0, 0.0)
@@ -271,9 +302,10 @@
             aug[h] = w.astype(BF)
             return 0
 
-        lax.fori_loop(0, KVH * GROUP, one, 0)
+        lax.fori_loop(k * GROUP, (k + 1) * GROUP, one, 0)
+        if k > 0:
+            return
         vcon[...] = jnp.where(both(lane >= 4, lane < 7), -1.0, 0.0).astype(BF)
-        dq_t[...] = jnp.zeros_like(dq_t)
         mine = layout[2 * b + p // 2]
         for role, owner in enumerate((b, d_from, blk(sib - 2), behind)):
             for s in range(2):
@@ -293,8 +325,8 @@
         for g in range(GROUP):
             h = k * GROUP + g
             lanes = pl.ds(pl.multiple_of(h * HD, HD), HD)
-            qs.append(q_ref[0, :, lanes])
-            gs.append(do_ref[0, :, lanes])
+            qs.append(q_ref[:, lanes])
+            gs.append(do_ref[:, lanes])
             w = aug[h]
             qa.append(jnp.concatenate([qs[-1], w], axis=1))
             ga.append(jnp.concatenate([gs[-1], w], axis=1))
@@ -311,18 +343,29 @@
         ds = (prob * nt(va, ga)).astype(BF)
         part[role, k, :, 1] = nn(prob.astype(BF), gs).reshape(LINE, rows, HD).astype(BF)
         part[role, k, :, 0] = nn(ds, qs).reshape(LINE, rows, HD).astype(BF)
-        dq_t[...] += tn(keys, ds)
+        kept[k, role] = ds
+
+    def dq_copy(k):
+        lanes = pl.ds(pl.multiple_of(k * GROUP * HD, GROUP * HD), GROUP * HD)
+        return pltpu.make_async_copy(dq_ref.at[:, lanes], dq_hbm.at[0, :, lanes], sem_out.at[k])
 
     def dq_out(k):
+        keys = got[:, k, :, 0].reshape(4 * keys_n, HD)
+        total = tn(keys, kept[k].reshape(4 * keys_n, GROUP * rows)) * (2 * SCALE)
         for g in range(GROUP):
             lanes = pl.ds(pl.multiple_of((k * GROUP + g) * HD, HD), HD)
-            tile = dq_t[:, g * rows:(g + 1) * rows] * SCALE
-            dq_ref[0, :, lanes] = tile.T.astype(BF)
-        dq_t[...] = jnp.zeros_like(dq_t)
-
+            dq_ref[:, lanes] = total[:, g * rows:(g + 1) * rows].T.astype(BF)
+        dq_copy(k).start()
+
+    loads = [
+        pltpu.make_async_copy(src.at[0], dst, sem_in.at[i])
+        for i, (src, dst) in enumerate(((do_hbm, do_ref), (o_hbm, o_ref), (q_hbm, q_ref)))
+    ]
     for k in range(KVH):
         own_copy(k, 0).start()
         own_copy(k, 1).start()
+    for load in loads:
+        load.start()
 
     barrier = pltpu.get_barrier_semaphore()
 
@@ -331,8 +374,8 @@
 
     greet(at(sib, p))
     greet(at(blk(b + 3 - 6 * (1 - core)), p))
-    pl.when(p > 0)(lambda: greet(at(b, p - 1)))
-    pl.when(p < LINE - 1)(lambda: greet(at(b, p + 1)))
+    for away in range(1, LINE):
+        greet(at(b, lax.rem(p + away, LINE)))
     at_end = jnp.logical_or(p == 0, p == LINE - 1)
 
     @pl.when(at_end)
@@ -340,69 +383,82 @@
         greet(at(ahead, 3 - p))
         greet(at(behind, 3 - p))
 
-    pl.semaphore_wait(barrier, jnp.where(at_end, 5, 4))
+    pl.semaphore_wait(barrier, jnp.where(at_end, 7, 5))
 
     own_send(0)
-    prepare()
+    own_send(1)
+    loads[0].wait()
+    loads[1].wait()
+    prepare(0)
     gather(0, 0)
-    own_send(1)
+    own_send(2)
+    prepare(1)
     gather(0, 1)
     gather(1, 0)
+    own_send(3)
+    prepare(2)
+    prepare(3)
     gather(0, 2)
+    gather(1, 1)
+    gather(2, 0)
+    c_d_all(0).start()
+    loads[2].wait()
 
     def when(cond, f):
         pl.when(cond)(f)
 
     def step(c, _):
-        i = lax.div(c, 4)
-        s = lax.rem(c, 4)
-
-        @pl.when(s == 0)
-        def _():
-            when(i < 3, lambda: gather(i + 1, 1))
-            when(i == 1, lambda: back(0, 0))
-
-        @pl.when(s == 1)
-        def _():
-            when(i == 0, lambda: gather(0, 3))
-            when(i < 3, lambda: gather(i + 1, 2))
-            when(i < 2, lambda: own_send(i + 2))
-            when(i >= 1, lambda: back(i - 1, 1))
-            when(i >= 2, lambda: back(i - 2, 3))
-
-        @pl.when(s == 3)
-        def _():
-            when(i < 3, lambda: gather(i + 1, 3))
-            when(i < 2, lambda: gather(i + 2, 0))
-            when(i >= 1, lambda: back(i, 0))
-            when(i >= 1, lambda: back(i - 1, 2))
-            when(i >= 2, lambda: back(i - 2, 4))
-
-        role = jnp.where(i == 0, s, jnp.where(s < 2, s + 2, 3 - s))
+        wave = lax.div(c + 5, 2)
+        for j in (3, 2, 1, 0):
+            k = wave - j
+            when(both(lax.rem(c, 2) == 1, k >= 0, k < KVH), lambda j=j, k=k: gather(k, j))
+        when(both(c > 0, c < 7, lax.rem(c, 2) == 0), lambda: c_d_all(lax.div(c, 2)).start())
+
+        def pick(*pairs):
+            out = pairs[-1]
+            for cond, value in reversed(pairs[:-1]):
+                out = jnp.where(cond, value, out)
+            return out
+
+        for t, gaps in enumerate(((5, 9, 13, 15), (9, 11, 14), (11, 13), (13, 15), (15,))):
+            k = pick(*((c == gap, k) for k, gap in enumerate(gaps)), -1)
+            when(k >= 0, lambda t=t, k=k: back(k, t))
+
+        i = pick((c >= 13, 3), (c >= 11, 2), (c == 10, 3), (c == 9, 2), (c >= 6, 1), (c == 5, 2), (c == 1, 1), 0)
+        role = pick(
+            (c == 15, 0), (c >= 11, 2 + lax.rem(c + 1, 2)), (c >= 9, 1), (c >= 6, lax.rem(c, 3) + 1),
+            (c == 4, 1), (jnp.logical_or(c == 2, c == 3), c), 0,
+        )
         when(role == 1, lambda: c_d_all(i).wait_recv())
         when(role == 2, lambda: c_sib_all(i).wait_recv())
         when(role == 0, lambda: chunk(i, 0, True))
         when(role > 0, lambda: chunk(i, role, False))
         when(role == 1, lambda: r_d(i).start())
         when(role == 2, lambda: r_sib(i).start())
-        when(s == 3, lambda: dq_out(i))
         return 0
 
     lax.fori_loop(0, 4 * KVH, step, 0)
-    back(3, 1)
+    back_last(1)
+    back(2, 2)
+
+    def queries_back(k, _):
+        dq_out(k)
+        return 0
+
+    lax.fori_loop(0, 2, queries_back, 0)
+    back(1, 4)
+    back_last(2)
     back(2, 3)
-    back(3, 2)
+    lax.fori_loop(2, KVH, queries_back, 0)
+    back_last(3)
     back(2, 4)
-    back(3, 3)
-    back(3, 4)
 
     def drain(k, _):
         for u in range(LINE):
             spread(k, u, wait_send)
             pass_on(k, u, wait_send)
             send_back(k, u, wait_send)
-            pl.when(u < p)(lambda: r_left(k, u).wait_send())
-            pl.when(u > p)(lambda: r_right(k, u).wait_send())
+            pl.when(u != p)(lambda: r_left(k, u).wait_send())
         c_d_all(k).wait_send()
         c_sib_all(k).wait_send()
         r_d(k).wait_send()
@@ -410,6 +466,8 @@
         return 0
 
     lax.fori_loop(0, KVH, drain, 0)
+    for k in range(KVH):
+        dq_copy(k).wait()
 
 
 def solution(mesh):
@@ -423,7 +481,7 @@
         sem = pltpu.SemaphoreType.DMA((KVH, LINE))
         sems = pltpu.SemaphoreType.DMA((KVH,))
         log_norm = jnp.transpose(log_norm, (0, 2, 1))
-        return pl.pallas_call(
+        twice = pl.pallas_call(
             functools.partial(kernel, n),
             out_shape=(
                 jax.ShapeDtypeStruct(queries.shape, BF),
@@ -431,26 +489,36 @@
                 jax.ShapeDtypeStruct(value_rows.shape, BF),
             ),
             in_specs=[
-                pl.BlockSpec(memory_space=pltpu.SMEM), vm, anywhere, anywhere, vm, vm, vm,
+                pl.BlockSpec(memory_space=pltpu.SMEM),
+            ] + [anywhere] * 5 + [
+                vm,
             ],
-            out_specs=(vm, vm, vm),
+            out_specs=(anywhere, vm, vm),
             scratch_shapes=[
+                pltpu.VMEM(queries.shape[1:], BF),
+                pltpu.VMEM(queries.shape[1:], BF),
+                pltpu.VMEM(queries.shape[1:], BF),
+                pltpu.VMEM(queries.shape[1:], BF),
+                pltpu.SemaphoreType.DMA((3,)),
+                sems,
                 pltpu.VMEM((4,) + unit, BF),
                 pltpu.VMEM((KVH * GROUP, rows, HD), BF),
                 pltpu.VMEM((4, LINE, rows, HD), BF),
                 pltpu.VMEM((rows, HD), BF),
-                pltpu.VMEM((HD, GROUP * rows), F32),
+                pltpu.VMEM((KVH, 4, LINE * rows, GROUP * rows), BF),
                 pltpu.VMEM((4,) + unit, BF),
                 pltpu.VMEM((2, rows, HD), F32),
             ]
             + [pltpu.VMEM(unit, BF)] * 8
+            + [pltpu.VMEM((LINE, 2, rows, HD), BF)]
             + [pltpu.SemaphoreType.DMA((KVH, 2))]
             + [sem] * 4 + [sems] * 2 + [sem] * 2 + [sems] * 2
-            + [sem] * 2 + [sems] * 2 + [sem] * 4 + [sems] * 2,
+            + [sem] * 2 + [sems] * 2 + [sem] * 4 + [sems] * 3,
             compiler_params=pltpu.CompilerParams(
                 collective_id=0, has_side_effects=True, vmem_limit_bytes=56 * 2**20
             ),
         )(block_layout, queries, key_rows, value_rows, attn_out, out_grad, log_norm)
+        return tuple(x * jnp.asarray(0.5, BF) for x in twice)
 
     placed = P("blk", "head", None)
     return jax.shard_map(

time: 92.9 us -> 84 us (0.904); the launches traced: 91 us -> 83.5 us
  Pallas kernels: 86.5 us -> 79.8 us
  local copies, waits for them, and re-layouts: 3.93 us -> 0.01 us
  other arithmetic: 0 us -> 3.05 us
    pallas_call x1, Pallas kernels: 86.5 us -> 79.8 us  [shards(): pl.pallas_call(functools.partial(kernel, n), out_shape=(jax.ShapeDtypeStr...]
    unnamed x7 -> x4, local copies, waits for them, and re-layouts: 3.93 us -> 0.01 us
    mul x0 -> x2, other arithmetic: none -> 3.05 us  [shards(): return tuple((x * jnp.asarray(0.5, BF) for x in twice))]
where the time goes in v2:
time: 84 us; the launch traced here: 83.5 us
  Pallas kernels  79.8 us (95%)
  other arithmetic  3.05 us (4%)
    pallas_call x1, Pallas kernels, shards(): pl.pallas_call(functools.partial(kernel, n), out_shape=(jax.ShapeDtypeStr...  79.8 us
    mul x2, other arithmetic, shards(): return tuple((x * jnp.asarray(0.5, BF) for x in twice))  3.05 us

profile of v2, /device:TPU:1, one launch (start us, length us, event | category | flops | bytes accessed | tf_op | source)
XLA Modules:
  0.0 83.5 jit_solution(8673338847588986627)
XLA Ops:
  0.6 79.8 %shard_map.94 = (bf16[1,128,4096]{2,1,0:T(8,128)(2,1)}, bf16[1,128,512]{2,1,0:T(8,128)(2,1)}, bf16[1,128,512]{2,1,0:T(8,128)(2,1)}) custom-call(s32[128]{0:T(128)} %layout.1, bf16[1,128,4096]{2,1,0:T(8,128)(2,1)} %q_hbm.1, bf16[1,128,512]{2,1,0:T(8,128)(2,1)} %k_hbm.1, bf16[1,128,512]{2,1,0:T(8,128)(2,1)} %v_hbm.1, bf16[1,128,4096]{2,1,0:T(8,128)(2,1)} %o_hbm.1, ...), custom_call_target="tpu_custom_call" | custom-call | tf_op jit(solution)/shard_map/pallas_call | solution.py:484
  80.4 0.0 copy-start
  80.4 0.0 copy-start.1
  80.5 2.3 %broadcast_multiply_fusion = bf16[1,128,4096]{2,1,0:T(8,128)(2,1)} fusion(bf16[1,128,4096]{2,1,0:T(8,128)(2,1)} %get-tuple-element.6), kind=kLoop, calls=%fused_computation | loop fusion | flops 524288 | bytes 2097152 | tf_op jit(solution)/shard_map/mul | solution.py:521
  82.8 0.0 copy-done
  82.8 0.0 copy-done.1
  82.8 0.7 broadcast_multiply_fusion.1
Async XLA Ops:
  80.4 2.4 %copy-start = (bf16[1,128,512]{2,1,0:T(8,128)(2,1)S(1)}, bf16[1,128,512]{2,1,0:T(8,128)(2,1)}, u32[]{:S(2)}) copy-start(bf16[1,128,512]{2,1,0:T(8,128)(2,1)} %get-tuple-element.7) | copy-start | bytes 393220
  80.4 2.3 %copy-start.1 = (bf16[1,128,512]{2,1,0:T(8,128)(2,1)S(1)}, bf16[1,128,512]{2,1,0:T(8,128)(2,1)}, u32[]{:S(2)}) copy-start(bf16[1,128,512]{2,1,0:T(8,128)(2,1)} %get-tuple-element.8) | copy-start | bytes 393220

commit v3 on v2

--- a/solution.py
+++ b/solution.py
@@ -19,6 +19,11 @@
 REACH = (0, 1, 3, 4)
 REACH_LAST = (1, 2, 2, 3)
 LAST = KVH - 1
+ORDER = (
+    (0, 0), (1, 0), (2, 0), (0, 2), (0, 3), (0, 1), (1, 2), (1, 3),
+    (1, 1), (2, 1), (2, 2), (2, 3), (3, 1), (3, 2), (3, 3), (3, 0),
+)
+BACK_GAPS = ((5, 8, 12, 15), (10, 13, 15), (12, 15), (14,), ())
 MESH = pl.DeviceIdType.MESH
 BF = jnp.bfloat16
 F32 = jnp.float32
@@ -393,26 +398,27 @@
     gather(0, 0)
     own_send(2)
     prepare(1)
-    gather(0, 1)
     gather(1, 0)
     own_send(3)
+    gather(0, 1)
+    gather(2, 0)
     prepare(2)
+    gather(1, 1)
+    gather(3, 0)
     prepare(3)
     gather(0, 2)
-    gather(1, 1)
-    gather(2, 0)
-    c_d_all(0).start()
+    gather(2, 1)
     loads[2].wait()
 
     def when(cond, f):
         pl.when(cond)(f)
 
     def step(c, _):
-        wave = lax.div(c + 5, 2)
-        for j in (3, 2, 1, 0):
-            k = wave - j
-            when(both(lax.rem(c, 2) == 1, k >= 0, k < KVH), lambda j=j, k=k: gather(k, j))
-        when(both(c > 0, c < 7, lax.rem(c, 2) == 0), lambda: c_d_all(lax.div(c, 2)).start())
+        for j in (3, 2, 1):
+            k = c + 4 - 2 * j
+            when(both(c > 0, k >= 0, k < KVH), lambda j=j, k=k: gather(k, j))
+        when(c == 1, lambda: c_d_all(0).start())
+        when(both(c >= 3, c <= 5), lambda: c_d_all(c - 2).start())
 
         def pick(*pairs):
             out = pairs[-1]
@@ -420,15 +426,15 @@
                 out = jnp.where(cond, value, out)
             return out
 
-        for t, gaps in enumerate(((5, 9, 13, 15), (9, 11, 14), (11, 13), (13, 15), (15,))):
+        for t, gaps in enumerate(BACK_GAPS):
             k = pick(*((c == gap, k) for k, gap in enumerate(gaps)), -1)
             when(k >= 0, lambda t=t, k=k: back(k, t))
 
-        i = pick((c >= 13, 3), (c >= 11, 2), (c == 10, 3), (c == 9, 2), (c >= 6, 1), (c == 5, 2), (c == 1, 1), 0)
-        role = pick(
-            (c == 15, 0), (c >= 11, 2 + lax.rem(c + 1, 2)), (c >= 9, 1), (c >= 6, lax.rem(c, 3) + 1),
-            (c == 4, 1), (jnp.logical_or(c == 2, c == 3), c), 0,
-        )
+        def table(entries):
+            return pick(*((c == at_c, v) for at_c, v in enumerate(entries)), entries[-1])
+
+        i = table([k for k, _ in ORDER])
+        role = table([r for _, r in ORDER])
         when(role == 1, lambda: c_d_all(i).wait_recv())
         when(role == 2, lambda: c_sib_all(i).wait_recv())
         when(role == 0, lambda: chunk(i, 0, True))
@@ -438,18 +444,19 @@
         return 0
 
     lax.fori_loop(0, 4 * KVH, step, 0)
-    back_last(1)
-    back(2, 2)
-
     def queries_back(k, _):
         dq_out(k)
         return 0
 
+    back(0, 4)
+    back_last(1)
+    back(1, 3)
+    back(2, 2)
     lax.fori_loop(0, 2, queries_back, 0)
     back(1, 4)
     back_last(2)
     back(2, 3)
-    lax.fori_loop(2, KVH, queries_back, 0)
+    lax.fori_loop(2, 4, queries_back, 0)
     back_last(3)
     back(2, 4)
 

time: 84 us -> 83.6 us (level)
  no operation moved by 1% of the time
where the time goes in v3:
time: 83.6 us; the launch traced here: 83.4 us
  Pallas kernels  79.7 us (95%)
  other arithmetic  3.05 us (4%)
    pallas_call x1, Pallas kernels, shards(): pl.pallas_call(functools.partial(kernel, n), out_shape=(jax.ShapeDtypeStr...  79.7 us
    mul x2, other arithmetic, shards(): return tuple((x * jnp.asarray(0.5, BF) for x in twice))  3.05 us

profile of v3, /device:TPU:1, one launch (start us, length us, event | category | flops | bytes accessed | tf_op | source)
XLA Modules:
  0.0 83.4 jit_solution(3498066742105794818)
XLA Ops:
  0.6 79.7 %shard_map.94 = (bf16[1,128,4096]{2,1,0:T(8,128)(2,1)}, bf16[1,128,512]{2,1,0:T(8,128)(2,1)}, bf16[1,128,512]{2,1,0:T(8,128)(2,1)}) custom-call(s32[128]{0:T(128)} %layout.1, bf16[1,128,4096]{2,1,0:T(8,128)(2,1)} %q_hbm.1, bf16[1,128,512]{2,1,0:T(8,128)(2,1)} %k_hbm.1, bf16[1,128,512]{2,1,0:T(8,128)(2,1)} %v_hbm.1, bf16[1,128,4096]{2,1,0:T(8,128)(2,1)} %o_hbm.1, ...), custom_call_target="tpu_custom_call" | custom-call | tf_op jit(solution)/shard_map/pallas_call | solution.py:491
  80.3 0.0 copy-start
  80.3 0.0 copy-start.1
  80.3 2.3 %broadcast_multiply_fusion = bf16[1,128,4096]{2,1,0:T(8,128)(2,1)} fusion(bf16[1,128,4096]{2,1,0:T(8,128)(2,1)} %get-tuple-element.6), kind=kLoop, calls=%fused_computation | loop fusion | flops 524288 | bytes 2097152 | tf_op jit(solution)/shard_map/mul | solution.py:528
  82.7 0.0 copy-done
  82.7 0.0 copy-done.1
  82.7 0.7 broadcast_multiply_fusion.1
Async XLA Ops:
  80.3 2.4 %copy-start = (bf16[1,128,512]{2,1,0:T(8,128)(2,1)S(1)}, bf16[1,128,512]{2,1,0:T(8,128)(2,1)}, u32[]{:S(2)}) copy-start(bf16[1,128,512]{2,1,0:T(8,128)(2,1)} %get-tuple-element.7) | copy-start | bytes 393220
  80.3 2.3 %copy-start.1 = (bf16[1,128,512]{2,1,0:T(8,128)(2,1)S(1)}, bf16[1,128,512]{2,1,0:T(8,128)(2,1)}, u32[]{:S(2)}) copy-start(bf16[1,128,512]{2,1,0:T(8,128)(2,1)} %get-tuple-element.8) | copy-start | bytes 393220
